TPU v7x, 256 devices: a whole 4x4x8 slice. The times are simulated.
256 devices in a mesh: role: 2 (over core), grp: 16 (over x, y), tp: 8 (over z).
Axes of the slice: x: 4, y: 4, z: 8, core: 2. Of those that a mesh axis runs over, the one named last changes fastest.
Arguments:
- queries: bfloat16 [2, 512, 6144], P('role', 'grp', 'tp'), may hold values from -7 to 7
- new_keys: bfloat16 [2, 512, 1024], P('role', 'grp', 'tp'), may hold values from -4 to 4
- new_values: bfloat16 [2, 512, 1024], P('role', 'grp', 'tp'), may hold values from -4 to 4
- cache_keys: bfloat16 [2, 512, 8, 256, 128], P('role', 'grp', 'tp'), may hold values from -4 to 4
- cache_values: bfloat16 [2, 512, 8, 256, 128], P('role', 'grp', 'tp'), may hold values from -4 to 4
- lengths: int32 [2, 512], P('role', 'grp'), may hold values from 1 to 256, as said below
- out_proj: bfloat16 [6144, 6144], P('tp', 'grp'), may hold values from -0.25 to 0.25
- residual: bfloat16 [2, 512, 6144], P('role', None, 'grp'), may hold values from -14 to 14
- norm_gain: float32 [6144], replicated, may hold values from 0.1 to 1.9
- expert_ids: int32 [2, 512, 2], replicated, may hold values from 0 to 7, all different within a row; in each aligned block of 512 rows (0 to 511, 512 to 1023, ..., all dimensions but the last counted through in order) at most 256 rows name the same one
- gate_weights: float32 [2, 512, 2], replicated, may hold values from 0.25 to 1
- expert_gate: bfloat16 [8, 6144, 8192], P('tp', None, ('role', 'grp')), may hold values from -0.078125 to 0.078125
- expert_up: bfloat16 [8, 6144, 8192], P('tp', None, ('role', 'grp')), may hold values from -0.078125 to 0.078125
- expert_down: bfloat16 [8, 8192, 6144], P('tp', 'role', 'grp'), may hold values from -0.0625 to 0.0625
Outputs:
- stream: bfloat16 [2, 512, 6144], P('role', None, 'grp')
- expert_mix: bfloat16 [2, 512, 6144], P('role', None, 'grp')
Inputs may be any that keep to these rules, and one draw needn't show every extreme that they name: `expert_ids`: the two experts of a token differ. Among the tokens of one micro-batch no expert is named more than 256 times, and in some micro-batch some expert is named exactly 256 times. `lengths`: cache positions at or past a sequence's length hold no data of it. Every micro-batch has a sequence of length 256.
All inputs are finite; a program needn't handle non-finite values.
Results may differ from a plain program's by a relative error of at most 0.02.
Values may be sent and summed in bfloat16 or wider, within the bound.
A program may use at most 128 MiB of HBM per device.

v0:
```python
import math

import jax
import jax.numpy as jnp
from jax import lax
from jax.sharding import PartitionSpec as P

D = 6144
EXPERTS = 8


def attend_local(queries, new_keys, new_values, cache_keys, cache_values, lengths):
    seqs = cache_keys.shape[1]
    kv_heads = cache_keys.shape[2]
    span = cache_keys.shape[3]
    head_dim = cache_keys.shape[4]
    group = queries.shape[2] // (kv_heads * head_dim)
    factor = 1.0 / math.sqrt(head_dim)
    query = queries[0].reshape(seqs, kv_heads, group, head_dim)
    fresh_key = new_keys[0].reshape(seqs, kv_heads, head_dim)
    fresh_value = new_values[0].reshape(seqs, kv_heads, head_dim)
    scores = (
        jnp.einsum("skgd,skpd->skgp", query, cache_keys[0], preferred_element_type=jnp.float32)
        * factor
    )
    fresh = (
        jnp.einsum("skgd,skd->skg", query, fresh_key, preferred_element_type=jnp.float32) * factor
    )
    valid = (jnp.arange(span, dtype=jnp.int32)[None, :] < lengths[0][:, None])[:, None, None, :]
    scores = jnp.where(valid, scores, -jnp.inf)
    highest = jnp.maximum(jnp.max(scores, axis=-1), fresh)
    weights = jnp.exp(scores - highest[..., None])
    own = jnp.exp(fresh - highest)
    denominator = jnp.sum(weights, axis=-1) + own
    probs = (weights / denominator[..., None]).astype(jnp.bfloat16)
    own_prob = (own / denominator).astype(jnp.bfloat16)
    mixed = jnp.einsum(
        "skgp,skpd->skgd", probs, cache_values[0], preferred_element_type=jnp.float32
    )
    mixed = (
        mixed
        + own_prob.astype(jnp.float32)[..., None] * fresh_value.astype(jnp.float32)[:, :, None, :]
    )
    return mixed.reshape(seqs, group * kv_heads * head_dim).astype(jnp.bfloat16)


def slot_tables(expert_ids, gate_weights, first_expert, local_count, capacity):
    micro, seqs, picks = expert_ids.shape
    routed = expert_ids.reshape(micro, seqs * picks)
    weight_flat = gate_weights.reshape(micro, seqs * picks)
    onehot = (routed[:, :, None] == jnp.arange(EXPERTS, dtype=jnp.int32)[None, None, :]).astype(
        jnp.int32
    )
    before = jnp.cumsum(onehot, axis=1) - onehot
    position = jnp.sum(before * onehot, axis=2)
    owned = first_expert + jnp.arange(local_count, dtype=jnp.int32)
    picked = (routed[:, None, None, :] == owned[None, :, None, None]) & (
        position[:, None, None, :] == jnp.arange(capacity, dtype=jnp.int32)[None, None, :, None]
    )
    token_index = jnp.arange(seqs * picks, dtype=jnp.int32) // picks
    which = jnp.sum(jnp.where(picked, token_index[None, None, None, :], 0), axis=3)
    weight = jnp.sum(jnp.where(picked, weight_flat[:, None, None, :], 0.0), axis=3)
    return (which, weight)


def add_at(accum, micro, term):
    current = lax.dynamic_slice_in_dim(accum, micro, 1, 1)
    return lax.dynamic_update_slice_in_dim(accum, current + term[:, None], micro, 1)


def absorb(carry, block, micro, column, expert_gate, expert_up, norm_gain):
    width = block.shape[-1]
    gain_part = lax.dynamic_slice_in_dim(norm_gain, column, width, 0)
    scaled = (block.astype(jnp.float32) * gain_part).astype(jnp.bfloat16)
    gate_part = lax.dynamic_slice_in_dim(expert_gate, column, width, 1)
    up_part = lax.dynamic_slice_in_dim(expert_up, column, width, 1)
    gate_term = jnp.einsum("ecd,edf->ecf", scaled, gate_part, preferred_element_type=jnp.float32)
    up_term = jnp.einsum("ecd,edf->ecf", scaled, up_part, preferred_element_type=jnp.float32)
    square_term = jnp.sum(jnp.square(block.astype(jnp.float32)), axis=-1)
    return (
        add_at(carry[0], micro, gate_term),
        add_at(carry[1], micro, up_term),
        add_at(carry[2], micro, square_term),
    )


def place_rows(rows_out, where_rows, scale_rows, seqs):
    local_count, capacity, width = rows_out.shape
    weighted = (rows_out * scale_rows[..., None]).reshape(local_count * capacity, width)
    return jax.ops.segment_sum(
        weighted, where_rows.reshape(local_count * capacity), num_segments=seqs
    )


def local(
    queries,
    new_keys,
    new_values,
    cache_keys,
    cache_values,
    lengths,
    out_proj,
    residual,
    norm_gain,
    expert_ids,
    gate_weights,
    expert_gate,
    expert_up,
    expert_down,
):
    attn = attend_local(queries, new_keys, new_values, cache_keys, cache_values, lengths)
    head_part = jnp.dot(
        lax.all_gather(attn, "grp", axis=0, tiled=True),
        out_proj,
        preferred_element_type=jnp.float32,
    )
    resid = residual[0]
    summed = lax.psum(head_part, "tp")
    stream = (resid.astype(jnp.float32) + summed).astype(jnp.bfloat16)
    micro_count, seqs, picks = expert_ids.shape
    capacity = seqs // 2
    local_count = expert_gate.shape[0]
    hidden_width = expert_gate.shape[2]
    width = stream.shape[1]
    groups = lax.axis_size("grp")
    role_index = lax.axis_index("role")
    which, weight = slot_tables(
        expert_ids, gate_weights, lax.axis_index("tp") * local_count, local_count, capacity
    )
    empty = jnp.zeros((local_count, micro_count, capacity, hidden_width), jnp.float32)
    start_carry = (empty, empty, jnp.zeros((local_count, micro_count, capacity), jnp.float32))
    carry = start_carry
    piece = lax.all_gather(stream[None], ("role", "grp"), axis=0, tiled=True)
    start = jnp.int32(0)
    for offset in range(piece.shape[0]):
        anchor = start + offset
        micro = anchor // groups
        table = lax.dynamic_index_in_dim(which, micro, 0, keepdims=False)
        block = jnp.take(piece[offset], table, axis=0)
        carry = absorb(
            carry, block, micro, anchor % groups * width, expert_gate, expert_up, norm_gain
        )
    gate_acc, up_acc, squares = carry
    rstat = (1.0 / jnp.sqrt(squares / D + 1e-05))[..., None]
    hidden = (jax.nn.silu(gate_acc * rstat) * (up_acc * rstat)).astype(jnp.bfloat16)
    hidden = hidden.reshape(local_count, micro_count * capacity, hidden_width)
    produced = jnp.einsum(
        "erf,efd->erd",
        lax.all_gather(hidden, "grp", axis=2, tiled=True),
        expert_down,
        preferred_element_type=jnp.float32,
    )
    produced = produced.reshape(local_count, micro_count, capacity, width)
    partial_mix = jnp.stack(
        [
            place_rows(produced[:, step], which[step], weight[step], seqs)
            for step in range(micro_count)
        ],
        axis=0,
    )
    summed_mix = lax.psum(partial_mix.astype(jnp.bfloat16), ("role", "tp")).astype(jnp.float32)
    expert_mix = lax.dynamic_slice_in_dim(summed_mix, role_index, 1, 0).astype(jnp.bfloat16)
    return (stream[None], expert_mix)


def solution(mesh):
    return jax.shard_map(
        local,
        mesh=mesh,
        in_specs=(
            P("role", "grp", "tp"),
            P("role", "grp", "tp"),
            P("role", "grp", "tp"),
            P("role", "grp", "tp", None, None),
            P("role", "grp", "tp", None, None),
            P("role", "grp"),
            P("tp", "grp"),
            P("role", None, "grp"),
            P(),
            P(),
            P(),
            P("tp", None, ("role", "grp")),
            P("tp", None, ("role", "grp")),
            P("tp", "role", "grp"),
        ),
        out_specs=(P("role", None, "grp"), P("role", None, "grp")),
        check_vma=False,
    )
```

profile of v0, /device:TPU:1, one launch (start us, length us, event | category | flops | bytes accessed | tf_op | source)
XLA Modules:
  0.0 547.2 jit_solution(4421056859976372559)
XLA Ops:
  15.3 20.3 %all_gather.9 = bf16[512,768]{1,0:T(8,128)(2,1)S(1)} all-gather(bf16[32,768]{1,0:T(8,128)(2,1)S(1)} %bitcast.1286), channel_id=1, replica_groups=mesh['role'=2,'grp'=16,'tp'=8] {'grp'}, dimensions={0}, use_global_device_ids=true | all-gather | bytes 835584 | tf_op jit(solution)/shard_map/all_gather | solution.py:113
  37.2 76.4 %all-reduce.6.cloned.1.call-done = f32[512,384]{1,0:T(8,128)} async-done(((f32[512,384]{1,0:T(8,128)}), f32[512,384]{1,0:T(8,128)}) %all-reduce.6.cloned.1.call-update) | async-done | bytes 786448 | tf_op jit(solution)/shard_map/psum | solution.py:118
  119.3 4.5 reduce-window.6
  127.1 61.1 %all-gather.6.cloned.1.call-done = bf16[16384,384]{1,0:T(8,128)(2,1)} async-done(((bf16[512,384]{1,0:T(8,128)(2,1)}), bf16[16384,384]{1,0:T(8,128)(2,1)}) %all-gather.6.cloned.1.call-update) | async-done | bytes 12582928 | tf_op jit(solution)/shard_map/all_gather | solution.py:133
  188.2 6.1 %fusion.440 = (bf16[512,384]{1,0:T(8,128)(2,1)}, bf16[512,384]{1,0:T(8,128)(2,1)}, bf16[512,384]{1,0:T(8,128)(2,1)}, bf16[512,384]{1,0:T(8,128)(2,1)}, bf16[512,...) fusion(bf16[16384,384]{1,0:T(8,128)(2,1)} %all-gather.6.cloned., ...), kind=kLoop, calls=%fused_computation.651 | loop fusion | bytes 14942208 | tf_op jit(solution)/shard_map/slice | solution.py:139
  197.1 2.9 gather_fusion.17
  202.9 2.9 gather_fusion.19
  205.7 2.9 gather_fusion.20
  220.0 2.9 gather_fusion.25
  237.1 3.3 gather_fusion.31
  240.4 2.9 gather_fusion.13
  243.3 2.9 gather_fusion.14
  247.9 4.7 fusion.441
  255.4 2.9 gather_fusion.3
  261.2 2.9 gather_fusion.5
  266.9 2.9 gather_fusion.7
  281.2 2.9 gather_fusion.12
  284.0 2.9 gather_fusion.1
  288.7 3.2 fusion.92
  354.5 58.0 %all-gather.4.cloned.1.call-done = bf16[1,512,4096]{2,1,0:T(8,128)(2,1)} async-done(((bf16[1,512,256]{2,1,0:T(8,128)(2,1)}), bf16[1,512,4096]{2,1,0:T(8,128)(2,1)}) %all-gather.4.cloned.1.call-update) | async-done | bytes 4194320 | tf_op jit(solution)/shard_map/all_gather | solution.py:149
  412.6 5.4 fusion.7
  418.0 3.7 scatter_custom_fusion
  421.7 3.7 scatter_custom_fusion.1
  427.8 110.9 %all-reduce.8.cloned.1.call-done = bf16[2,512,384]{2,1,0:T(8,128)(2,1)} async-done(((bf16[2,512,384]{2,1,0:T(8,128)(2,1)}), bf16[2,512,384]{2,1,0:T(8,128)(2,1)}) %all-reduce.8.cloned.1.call-update) | async-done | bytes 786448 | tf_op jit(solution)/shard_map/psum | solution.py:161
  (293 shorter events, 139.0 us)
Async XLA Ops:
  7.2 405.4 %copy-start = (bf16[1,4096,384]{2,1,0:T(8,128)(2,1)S(1)}, bf16[1,4096,384]{2,1,0:T(8,128)(2,1)}, u32[]{:S(2)}) copy-start(bf16[1,4096,384]{2,1,0:T(8,128)(2,1)} %param.29) | copy-start | bytes 9437188
  7.2 106.4 %all-reduce.6.cloned.1.call-start = ((), (), s32[]{:S(2)}) async-start(), calls=%async_computation | async-start | bytes 1572864 | tf_op jit(solution)/shard_map/psum | solution.py:118
  9.8 25.8 %copy-start.35 = (bf16[768,384]{1,0:T(8,128)(2,1)S(1)}, bf16[768,384]{1,0:T(8,128)(2,1)}, u32[]{:S(2)}) copy-start(bf16[768,384]{1,0:T(8,128)(2,1)} %param.22) | copy-start | bytes 1769476
  13.2 100.4 %copy-start.36 = (bf16[1,512,384]{2,1,0:T(8,128)(2,1)S(1)}, bf16[1,512,384]{2,1,0:T(8,128)(2,1)}, u32[]{:S(2)}) copy-start(bf16[1,512,384]{2,1,0:T(8,128)(2,1)} %param.23) | copy-start | bytes 1179652
  15.3 100.3 %copy-start.60 = (s32[2,512,2]{1,2,0:T(2,128)S(1)}, s32[2,512,2]{1,2,0:T(2,128)}, u32[]{:S(2)}) copy-start(s32[2,512,2]{1,2,0:T(2,128)} %param.25) | copy-start | bytes 24580
  37.1 151.1 %all-gather.6.cloned.1.call-start = ((), (), s32[]{:S(2)}) async-start(), calls=%async_computation.3 | async-start | bytes 12976128 | tf_op jit(solution)/shard_map/all_gather | solution.py:133
  115.5 297.0 %all-gather.4.cloned.1.call-start = ((), (), s32[]{:S(2)}) async-start(), calls=%async_computation.1 | async-start | bytes 4456448 | tf_op jit(solution)/shard_map/all_gather | solution.py:149
  288.7 14.0 %copy-start.3 = (bf16[256,384]{1,0:T(8,128)(2,1)S(1)}, bf16[256,384]{1,0:T(8,128)(2,1)}, u32[]{:S(2)}) copy-start(bf16[256,384]{1,0:T(8,128)(2,1)} %gather_fusion.31) | copy-start | bytes 589828
  288.7 14.0 %copy-start.4 = (bf16[256,384]{1,0:T(8,128)(2,1)S(1)}, bf16[256,384]{1,0:T(8,128)(2,1)}, u32[]{:S(2)}) copy-start(bf16[256,384]{1,0:T(8,128)(2,1)} %gather_fusion.16) | copy-start | bytes 589828
  302.7 29.0 %copy-start.51 = (f32[384]{0:T(512)S(1)}, f32[384]{0:T(512)}, u32[]{:S(2)}) copy-start(f32[384]{0:T(512)} %get-tuple-element.115) | copy-start | bytes 4612
  305.6 26.5 %copy-start.50 = (f32[384]{0:T(512)S(1)}, f32[384]{0:T(512)}, u32[]{:S(2)}) copy-start(f32[384]{0:T(512)} %get-tuple-element.114) | copy-start | bytes 4612
  326.6 5.2 copy-start.1
  326.6 5.2 copy-start.31
  326.6 5.5 %copy-start.30 = (bf16[256,384]{1,0:T(8,128)(2,1)S(1)}, bf16[256,384]{1,0:T(8,128)(2,1)}, u32[]{:S(2)}) copy-start(bf16[256,384]{1,0:T(8,128)(2,1)} %gather_fusion.4) | copy-start | bytes 589828
  327.4 5.1 copy-start.29
  327.4 5.1 copy-start.49
  329.0 3.7 copy-start.28
  329.0 3.7 copy-start.48
  330.4 2.7 copy-start.27
  330.4 2.7 copy-start.47
  349.7 4.3 copy-start.38
  349.7 4.3 copy-start.55
  349.7 4.8 copy-start.58
  351.5 187.2 %all-reduce.8.cloned.1.call-start = ((), (), s32[]{:S(2)}) async-start(), calls=%async_computation.2 | async-start | bytes 1572864 | tf_op jit(solution)/shard_map/psum | solution.py:161
  (42 other events, 69.2 us)
Sparse Core Ops, SparseCore 0:
  37.2 76.2 all-reduce.5
  117.1 71.1 all-gather.5
  351.6 60.8 all-gather.3
  428.0 110.6 all-reduce.7
where the time goes:
time: 553 us; the launch traced here: 547 us
  waiting for transfers between devices  306 us (55%)
  local copies, waits for them, and re-layouts  140 us (25%)
  matrix products  33.5 us (6%)
  other arithmetic  31.2 us (6%)
  blocking collectives  20.3 us (4%)
  between operations  15.5 us (3%)
    psum x1, waiting for transfers between devices, local(): lax.psum(partial_mix.astype(jnp.bfloat16), ('role', 'tp'))  111 us
    gather x32, local copies, waits for them, and re-layouts, local(): block = jnp.take(piece[offset], table, axis=0)  89.8 us
    psum x1, waiting for transfers between devices, local(): summed = lax.psum(head_part, 'tp')  76.4 us
    all_gather x1, waiting for transfers between devices, local(): piece = lax.all_gather(stream[None], ('role', 'grp'), axis=0, tiled=True)  61.1 us
    all_gather x1, waiting for transfers between devices, local(): lax.all_gather(hidden, 'grp', axis=2, tiled=True)  58 us
    dynamic_update_slice x36, local copies, waits for them, and re-layouts, add_at(): lax.dynamic_update_slice_in_dim(accum, current + term[:, None], micro, 1)  29.3 us
    all_gather x1, blocking collectives, local(): lax.all_gather(attn, 'grp', axis=0, tiled=True)  20.3 us
    dot_general x32, matrix products, absorb(): jnp.einsum('ecd,edf->ecf', scaled, gate_part, preferred_element_type=jnp....  12.3 us
  transfers between devices with their start and end apart: 4, of which 4 were waited for; matrix products, arithmetic and copies ran while one was open for 3% of the time, Pallas kernels for 0%

commit v1 on v0

v1 whole, which is shorter than its diff:
```python
import math

import jax
import jax.numpy as jnp
from jax import lax
from jax.experimental import pallas as pl
from jax.experimental.pallas import tpu as pltpu
from jax.sharding import PartitionSpec as P

MESH = pl.DeviceIdType.MESH
BF16 = jnp.bfloat16
F32 = jnp.float32
D = 6144
SIDE = 4
GROUPS = 16
PLANES = 8


def attend_local(queries, new_keys, new_values, cache_keys, cache_values, lengths):
    seqs = cache_keys.shape[1]
    kv_heads = cache_keys.shape[2]
    span = cache_keys.shape[3]
    head_dim = cache_keys.shape[4]
    group = queries.shape[2] // (kv_heads * head_dim)
    factor = 1.0 / math.sqrt(head_dim)
    query = queries[0].reshape(seqs, kv_heads, group, head_dim)
    fresh_key = new_keys[0].reshape(seqs, kv_heads, head_dim)
    fresh_value = new_values[0].reshape(seqs, kv_heads, head_dim)
    scores = (
        jnp.einsum("skgd,skpd->skgp", query, cache_keys[0], preferred_element_type=jnp.float32)
        * factor
    )
    fresh = (
        jnp.einsum("skgd,skd->skg", query, fresh_key, preferred_element_type=jnp.float32) * factor
    )
    valid = (jnp.arange(span, dtype=jnp.int32)[None, :] < lengths[0][:, None])[:, None, None, :]
    scores = jnp.where(valid, scores, -jnp.inf)
    highest = jnp.maximum(jnp.max(scores, axis=-1), fresh)
    weights = jnp.exp(scores - highest[..., None])
    own = jnp.exp(fresh - highest)
    denominator = jnp.sum(weights, axis=-1) + own
    probs = (weights / denominator[..., None]).astype(jnp.bfloat16)
    own_prob = (own / denominator).astype(jnp.bfloat16)
    mixed = jnp.einsum(
        "skgp,skpd->skgd", probs, cache_values[0], preferred_element_type=jnp.float32
    )
    mixed = (
        mixed
        + own_prob.astype(jnp.float32)[..., None] * fresh_value.astype(jnp.float32)[:, :, None, :]
    )
    return mixed.reshape(seqs, group * kv_heads * head_dim).astype(jnp.bfloat16)


def remote(src, dst, send_sem, recv_sem, device):
    return pltpu.make_async_remote_copy(
        src_ref=src,
        dst_ref=dst,
        send_sem=send_sem,
        recv_sem=recv_sem,
        device_id=device,
        device_id_type=MESH,
    )


class PlaneGather:
    def __init__(self, place, piece, send, recv):
        self.place, self.piece, self.send, self.recv = place, piece, send, recv

    def at(self, half, first, second):
        role, x, y, plane = self.place
        dx, dy = (first, second) if half == 0 else (second, first)
        return lax.rem(x + dx, SIDE) * SIDE + lax.rem(y + dy, SIDE)

    def copy(self, half, first, phase, step):
        role, x, y, plane = self.place
        piece = self.piece(self.at(half, first, 0), half)
        if phase == 0:
            target = self.at(half, step, 0)
            send, recv = self.send.at[half, SIDE, step], self.recv.at[half, SIDE - step, 0]
        else:
            target = self.at(half, 0, step)
            send, recv = self.send.at[half, first, step], self.recv.at[half, first, SIDE - step]
        return remote(piece, piece, send, recv, (role, target, plane))

    def wait(self, half, first, second):
        role, x, y, plane = self.place
        piece = self.piece(self.at(half, first, second), half)
        remote(
            piece, piece, self.send.at[half, 0, 0], self.recv.at[half, first, second], (role, 0, plane)
        ).wait_recv()

    def start(self, halves=(0, 1)):
        for step in (1, 3, 2):
            for half in halves:
                self.copy(half, 0, 0, step).start()
        for step in (1, 3, 2):
            for half in halves:
                self.copy(half, 0, 1, step).start()

    def forward(self):
        for first in (1, 3, 2):
            for half in (0, 1):
                self.wait(half, first, 0)
                for step in (1, 3, 2):
                    self.copy(half, first, 1, step).start()

    def finish(self):
        def body(step, carry):
            for half in (0, 1):
                self.copy(half, 0, 0, step).wait_send()
                for first in range(SIDE):
                    self.copy(half, first, 1, step).wait_send()
            return carry

        lax.fori_loop(1, SIDE, body, 0)


def layer(
    attn_ref,
    proj_hbm,
    resid_ref,
    gain_ref,
    ids_ref,
    gates_ref,
    gate_hbm,
    up_hbm,
    down_hbm,
    stream_ref,
    mix_ref,
    attn_all,
    proj,
    gate_w,
    up_w,
    down_w,
    heads,
    head_in,
    rows_all,
    gate_acc,
    up_acc,
    square_acc,
    hidden_all,
    down_acc,
    half_out,
    half_in,
    mix_part,
    mix_in,
    pick,
    place_t,
    weight_col,
    load_sem,
    attn_send,
    attn_recv,
    rows_send,
    rows_recv,
    hid_send,
    hid_recv,
    sib_send,
    sib_recv,
    z_send,
    z_recv,
):
    role = lax.axis_index("role")
    grp = lax.axis_index("grp")
    plane = lax.axis_index("tp")
    x, y = grp // SIDE, lax.rem(grp, SIDE)
    place = (role, x, y, plane)
    sibling = (1 - role, grp, plane)

    def along_z(step):
        return (role, grp, lax.rem(plane + step, PLANES))

    loads = [
        pltpu.make_async_copy(src, dst, load_sem.at[i])
        for i, (src, dst) in enumerate(
            ((proj_hbm, proj), (gate_hbm, gate_w), (up_hbm, up_w), (down_hbm, down_w))
        )
    ]
    for load in loads:
        load.start()

    barrier = pltpu.get_barrier_semaphore()
    near = [(role, lax.rem(x + k, SIDE) * SIDE + y, plane) for k in (1, 2, 3)]
    near += [(role, x * SIDE + lax.rem(y + k, SIDE), plane) for k in (1, 2, 3)]
    near += [along_z(k) for k in range(1, PLANES)] + [sibling]
    for device in near:
        pl.semaphore_signal(barrier, inc=1, device_id=device, device_id_type=MESH)
    pl.semaphore_wait(barrier, len(near))

    attn_all[pl.ds(grp * 32, 32), :] = attn_ref[...]
    attn = PlaneGather(
        place, lambda g, half: attn_all.at[pl.ds(g * 32 + half * 16, 16)], attn_send, attn_recv
    )
    attn.start()

    ids = ids_ref[role]
    hit0, hit1 = ids[0:1, :] == plane, ids[1:2, :] == plane
    named = jnp.where(hit0 | hit1, 1.0, 0.0)
    gates = gates_ref[role]
    weight_row = jnp.where(hit0, gates[0:1, :], gates[1:2, :])
    seqs = named.shape[1]
    slots = pick.shape[0]
    earlier = lax.broadcasted_iota(jnp.int32, (seqs, seqs), 0) < lax.broadcasted_iota(
        jnp.int32, (seqs, seqs), 1
    )
    before = jnp.dot(
        jnp.broadcast_to(named, (16, seqs)).astype(BF16),
        jnp.where(earlier, 1.0, 0.0).astype(BF16),
        preferred_element_type=F32,
    )[0:1, :]
    slot = jnp.where(named > 0.5, before, -1.0).astype(jnp.int32)
    chosen = jnp.where(
        slot == lax.broadcasted_iota(jnp.int32, (slots, seqs), 0), 1.0, 0.0
    )
    pick[...] = chosen.astype(BF16)
    place_t[...] = chosen.T.astype(BF16)
    weight_col[...] = jnp.broadcast_to(
        jnp.sum(chosen * weight_row, axis=1, keepdims=True), weight_col.shape
    )
    gate_acc[...] = jnp.zeros_like(gate_acc)
    up_acc[...] = jnp.zeros_like(up_acc)
    square_acc[...] = jnp.zeros_like(square_acc)
    down_acc[...] = jnp.zeros_like(down_acc)

    attn.forward()

    def attn_rest(s, carry):
        attn.wait(0, 0, s)
        attn.wait(1, 0, s)
        for first in range(1, SIDE):
            attn.wait(0, first, s)
            attn.wait(1, first, s)
        return carry

    lax.fori_loop(1, SIDE, attn_rest, 0)
    loads[0].wait()

    def project(i, carry):
        part = jnp.dot(attn_all[pl.ds(i * 256, 256), :], proj[...], preferred_element_type=F32)
        heads[pl.ds(i * 256, 256), :] = part.astype(BF16)
        return carry

    lax.fori_loop(0, 2, project, 0)

    mine = pl.ds(plane * 64, 64)

    def scatter(src, dst, s):
        def one(step):
            to = lax.rem(plane + step, PLANES)
            return remote(
                src.at[pl.ds(to * 64, 64)],
                dst.at[step],
                z_send.at[s, step],
                z_recv.at[s, step],
                along_z(step),
            )

        def go(step, carry):
            one(step).start()
            return carry

        def arrive(step, carry):
            one(step).wait_recv()
            return carry + dst[step].astype(F32)

        lax.fori_loop(1, PLANES, go, 0)
        return lax.fori_loop(1, PLANES, arrive, src[mine, :].astype(F32)), one

    def spread(ref, s):
        def one(step, owner):
            block = ref.at[pl.ds(owner * 64, 64)]
            return remote(block, block, z_send.at[s, step], z_recv.at[s, step], along_z(step))

        def go(step, carry):
            one(step, plane).start()
            return carry

        def arrive(step, carry):
            one(step, lax.rem(plane + PLANES - step, PLANES)).wait_recv()
            return carry

        lax.fori_loop(1, PLANES, go, 0)
        lax.fori_loop(1, PLANES, arrive, 0)
        return lambda step: one(step, plane)

    summed, heads_copy = scatter(heads, head_in, 0)
    stream_ref[mine, :] = (resid_ref[mine, :].astype(F32) + summed).astype(BF16)
    stream_copy = spread(stream_ref, 1)

    gain = gain_ref[pl.ds(grp, 1), :]
    scaled = (stream_ref[...].astype(F32) * gain).astype(BF16)
    rows_all[role, grp] = jnp.dot(pick[...], scaled, preferred_element_type=F32).astype(BF16)
    rows = PlaneGather(
        place,
        lambda g, half: rows_all.at[role, g, pl.ds(half * 128, 128)],
        rows_send,
        rows_recv,
    )
    rows.start()

    def block_at(dx, dy):
        return lax.rem(x + dx, SIDE) * SIDE + lax.rem(y + dy, SIDE)

    def sibling_copy(dx, dy):
        block = rows_all.at[role, block_at(dx, dy)]
        return remote(block, block, sib_send.at[dx, dy], sib_recv.at[dx, dy], sibling)

    def sibling_wait(dx, dy):
        block = rows_all.at[1 - role, block_at(dx, dy)]
        remote(block, block, sib_send.at[dx, dy], sib_recv.at[dx, dy], sibling).wait_recv()

    sibling_copy(0, 0).start()
    loads[1].wait()
    loads[2].wait()

    def expert_in(dx, dy):
        g = block_at(dx, dy)
        depth = pl.ds(pl.multiple_of(g * 384, 128), 384)
        inverse = 1.0 / gain_ref[pl.ds(g, 1), :]
        for micro in range(2):
            block = rows_all[micro, g]
            into = pl.ds(micro * 256, 256)
            gate_acc[into, :] += jnp.dot(block, gate_w[depth, :], preferred_element_type=F32)
            up_acc[into, :] += jnp.dot(block, up_w[depth, :], preferred_element_type=F32)
            plain = block.astype(F32) * inverse
            plain = plain * plain
            square_acc[into, :] += plain[:, :128] + plain[:, 128:256] + plain[:, 256:]

    rows.forward()
    sibling_wait(0, 0)
    expert_in(0, 0)

    def row_axis(s, carry):
        rows.wait(1, 0, s)
        sibling_copy(s, 0).start()
        rows.wait(0, 0, s)
        sibling_copy(0, s).start()
        sibling_wait(s, 0)
        expert_in(s, 0)
        sibling_wait(0, s)
        expert_in(0, s)
        return carry

    lax.fori_loop(1, SIDE, row_axis, 0)

    def row_rest(s, carry):
        dx, dy = 1 + s // 3, 1 + lax.rem(s, 3)
        rows.wait(0, dx, dy)
        rows.wait(1, dy, dx)
        sibling_copy(dx, dy).start()
        sibling_wait(dx, dy)
        expert_in(dx, dy)
        return carry

    lax.fori_loop(0, 9, row_rest, 0)

    hid = PlaneGather(
        place, lambda g, half: hidden_all.at[g, pl.ds(half * 256, 256)], hid_send, hid_recv
    )
    for micro in range(2):
        into = pl.ds(micro * 256, 256)
        mean = jnp.sum(square_acc[into, :], axis=1, keepdims=True) / D
        rstat = 1.0 / jnp.sqrt(mean + 1e-05)
        act = gate_acc[into, :] * rstat
        hidden_all[grp, into, :] = (act / (1.0 + jnp.exp(-act)) * (up_acc[into, :] * rstat)).astype(
            BF16
        )
        hid.start((micro,))
    loads[3].wait()

    def expert_out(dx, dy):
        g = block_at(dx, dy)
        depth = pl.ds(pl.multiple_of(g * 256, 256), 256)
        for micro in range(2):
            into = pl.ds(micro * 256, 256)
            down_acc[into, :] += jnp.dot(
                hidden_all[g, into, :], down_w[depth, :], preferred_element_type=F32
            )

    hid.forward()
    expert_out(0, 0)

    def hid_axis(s, carry):
        hid.wait(1, 0, s)
        expert_out(s, 0)
        hid.wait(0, 0, s)
        expert_out(0, s)
        return carry

    lax.fori_loop(1, SIDE, hid_axis, 0)

    def hid_rest(s, carry):
        dx, dy = 1 + s // 3, 1 + lax.rem(s, 3)
        hid.wait(0, dx, dy)
        hid.wait(1, dy, dx)
        expert_out(dx, dy)
        return carry

    lax.fori_loop(0, 9, hid_rest, 0)

    half_out[...] = down_acc[pl.ds((1 - role) * 256, 256), :].astype(BF16)
    exchange = remote(half_out, half_in, sib_send.at[0, 4], sib_recv.at[0, 4], sibling)
    exchange.start()
    exchange.wait_recv()
    whole = down_acc[pl.ds(role * 256, 256), :] + half_in[...].astype(F32)
    weighted = (whole * weight_col[:, 0:1]).astype(BF16)
    mix_part[...] = jnp.dot(place_t[...], weighted, preferred_element_type=F32).astype(BF16)
    total, mix_copy = scatter(mix_part, mix_in, 2)
    mix_ref[mine, :] = total.astype(BF16)
    out_copy = spread(mix_ref, 3)

    attn.finish()
    rows.finish()
    hid.finish()
    exchange.wait_send()

    def sent_z(step, carry):
        heads_copy(step).wait_send()
        stream_copy(step).wait_send()
        mix_copy(step).wait_send()
        out_copy(step).wait_send()
        return carry

    lax.fori_loop(1, PLANES, sent_z, 0)

    def sent_sibling(s, carry):
        sibling_copy(s // SIDE, lax.rem(s, SIDE)).wait_send()
        return carry

    lax.fori_loop(0, GROUPS, sent_sibling, 0)


def local(
    queries,
    new_keys,
    new_values,
    cache_keys,
    cache_values,
    lengths,
    out_proj,
    residual,
    norm_gain,
    expert_ids,
    gate_weights,
    expert_gate,
    expert_up,
    expert_down,
):
    attn = attend_local(queries, new_keys, new_values, cache_keys, cache_values, lengths)
    vmem = pl.BlockSpec(memory_space=pltpu.VMEM)
    hbm = pl.BlockSpec(memory_space=pl.ANY)
    dma = pltpu.SemaphoreType.DMA
    stream, mix = pl.pallas_call(
        layer,
        out_shape=(
            jax.ShapeDtypeStruct((512, 384), BF16),
            jax.ShapeDtypeStruct((512, 384), BF16),
        ),
        in_specs=[vmem, hbm, vmem, vmem, vmem, vmem, hbm, hbm, hbm],
        out_specs=(vmem, vmem),
        scratch_shapes=[
            pltpu.VMEM((512, 768), BF16),
            pltpu.VMEM((768, 384), BF16),
            pltpu.VMEM((6144, 256), BF16),
            pltpu.VMEM((6144, 256), BF16),
            pltpu.VMEM((4096, 384), BF16),
            pltpu.VMEM((512, 384), BF16),
            pltpu.VMEM((8, 64, 384), BF16),
            pltpu.VMEM((2, 16, 256, 384), BF16),
            pltpu.VMEM((512, 256), F32),
            pltpu.VMEM((512, 256), F32),
            pltpu.VMEM((512, 128), F32),
            pltpu.VMEM((16, 512, 256), BF16),
            pltpu.VMEM((512, 384), F32),
            pltpu.VMEM((256, 384), BF16),
            pltpu.VMEM((256, 384), BF16),
            pltpu.VMEM((512, 384), BF16),
            pltpu.VMEM((8, 64, 384), BF16),
            pltpu.VMEM((256, 512), BF16),
            pltpu.VMEM((512, 256), BF16),
            pltpu.VMEM((256, 128), F32),
            dma((4,)),
            dma((2, 5, 4)),
            dma((2, 4, 4)),
            dma((2, 5, 4)),
            dma((2, 4, 4)),
            dma((2, 5, 4)),
            dma((2, 4, 4)),
            dma((4, 5)),
            dma((4, 5)),
            dma((4, 8)),
            dma((4, 8)),
        ],
        compiler_params=pltpu.CompilerParams(
            collective_id=0, has_side_effects=True, vmem_limit_bytes=48 << 20
        ),
    )(
        attn,
        out_proj,
        residual[0],
        norm_gain.reshape(16, 384),
        jnp.swapaxes(expert_ids, 1, 2),
        jnp.swapaxes(gate_weights, 1, 2),
        expert_gate[0],
        expert_up[0],
        expert_down[0],
    )
    return (stream[None], mix[None])


def solution(mesh):
    return jax.shard_map(
        local,
        mesh=mesh,
        in_specs=(
            P("role", "grp", "tp"),
            P("role", "grp", "tp"),
            P("role", "grp", "tp"),
            P("role", "grp", "tp", None, None),
            P("role", "grp", "tp", None, None),
            P("role", "grp"),
            P("tp", "grp"),
            P("role", None, "grp"),
            P(),
            P(),
            P(),
            P("tp", None, ("role", "grp")),
            P("tp", None, ("role", "grp")),
            P("tp", "role", "grp"),
        ),
        out_specs=(P("role", None, "grp"), P("role", None, "grp")),
        check_vma=False,
    )
```

time: 553 us -> 142 us (0.26)
  waiting for transfers between devices: 306 us -> 0 us
  local copies, waits for them, and re-layouts: 140 us -> 3.17 us
  Pallas kernels: 0 us -> 131 us
  matrix products: 33.5 us -> 3.9 us
  other arithmetic: 31.2 us -> 1.79 us
  blocking collectives: 20.3 us -> 0 us
  between operations: 15.5 us -> 0.75 us
    psum x2 -> x0, waiting for transfers between devices: 187 us -> none  [the longest x1 111 us: local(): lax.psum(partial_mix.astype(jnp.bfloat16), ('role', 'tp'))]
    pallas_call x0 -> x1, Pallas kernels: none -> 131 us  [local(): pl.pallas_call(layer, out_shape=(jax.ShapeDtypeStruct((512, 384), BF16),...]
    all_gather x2 -> x0, waiting for transfers between devices: 119 us -> none  [the longest x1 61.1 us: local(): piece = lax.all_gather(stream[None], ('role', 'grp'), axis=0, tiled=True)]
    gather x32 -> x0, local copies, waits for them, and re-layouts: 89.8 us -> none  [local(): block = jnp.take(piece[offset], table, axis=0)]
    dynamic_update_slice x36 -> x0, local copies, waits for them, and re-layouts: 29.3 us -> none  [add_at(): lax.dynamic_update_slice_in_dim(accum, current + term[:, None], micro, 1)]
    dot_general x66 -> x0, matrix products: 28.2 us -> none  [the longest x32 12.3 us: absorb(): jnp.einsum('ecd,edf->ecf', scaled, gate_part, preferred_element_type=jnp....]
    all_gather x1 -> x0, blocking collectives: 20.3 us -> none  [local(): lax.all_gather(attn, 'grp', axis=0, tiled=True)]
    slice x5 -> x0, local copies, waits for them, and re-layouts: 11.1 us -> none  [the longest x2 10.7 us: local(): block = jnp.take(piece[offset], table, axis=0)]
  transfers between devices with their start and end apart: 4 -> 0, of which waited for: 4 -> 0; matrix products, arithmetic and copies ran while one was open for 3% -> 0% of each run, Pallas kernels for 0% -> 0%
where the time goes in v1:
time: 142 us; the launch traced here: 140 us
  Pallas kernels  131 us (92%)
  matrix products  3.9 us (3%)
  local copies, waits for them, and re-layouts  3.17 us (2%)
  other arithmetic  1.79 us (1%)
    pallas_call x1, Pallas kernels, local(): pl.pallas_call(layer, out_shape=(jax.ShapeDtypeStruct((512, 384), BF16),...  131 us

profile of v1, /device:TPU:1, one launch (start us, length us, event | category | flops | bytes accessed | tf_op | source)
XLA Modules:
  0.0 140.4 jit_solution(3507496091784177504)
XLA Ops:
  0.6 0.0 copy-start
  0.6 0.9 iota_compare_fusion
  1.5 0.7 bitcast_convert_fusion
  2.2 0.7 reshape.105.gain_ref
  3.0 0.9 reshape.101
  3.8 0.9 fusion.19
  4.7 0.0 copy-done
  4.7 0.0 copy-start.1
  4.7 0.7 fusion.23
  5.5 0.0 copy-start.2
  5.5 0.0 copy-start.3
  5.5 0.0 copy-start.4
  5.5 0.0 copy-start.5
  5.5 0.2 fusion.16
  5.7 2.3 %fusion.13 = bf16[32,6,128]{2,1,0:T(8,128)(2,1)S(1)} fusion(bf16[1,32,1,256,128]{4,3,2,1,0:T(8,128)(2,1)} %param.18, f32[32,6,256]{2,1,0:T(8,128)S(1)} %get-tuple-element.9, f32[32,6]{1,0:T(8,128)S(1)} %get-tuple-element.7, f32[32,6]{1,0:T(8,128)S(1)} %multiply_maximum_fusion, f32[32,128]{1,0:T(8,128)S(1)} %bitcast_convert_fusion, ...), kind=kOutput, calls=%fused_computation.7 | convolution fusion | flops 12804096 | bytes 2361600 | tf_op jit(solution)/shard_map/skgp,skpd->skgd/dot_general | solution.py:44
  8.1 0.0 copy-done.1
  8.1 0.0 copy-done.2
  8.1 0.0 copy-done.3
  8.1 0.0 copy-done.4
  8.1 0.0 copy-done.5
  8.1 130.8 %shard_map.149 = (bf16[512,384]{1,0:T(8,128)(2,1)S(1)}, bf16[512,384]{1,0:T(8,128)(2,1)S(1)}) custom-call(bf16[32,768]{1,0:T(8,128)(2,1)S(1)} %bitcast.42, bf16[768,384]{1,0:T(8,128)(2,1)S(1)} %copy-done.2, bf16[512,384]{1,0:T(8,128)(2,1)S(1)} %bitcast.39, f32[16,384]{1,0:T(8,128)S(1)} %reshape.105.gain_ref, s32[2,2,512]{2,1,0:T(2,128)S(1)} %bitcast.43, ...), custom_call_target="tpu_custom_call" | custom-call | tf_op jit(solution)/shard_map/pallas_call | solution.py:452
  139.0 0.7 copy.25
  139.7 0.7 copy.26
  (3 shorter events, 0.0 us)
Async XLA Ops:
  0.6 4.1 %copy-start = (bf16[1,32,1,256,128]{4,3,2,1,0:T(8,128)(2,1)S(1)}, bf16[1,32,1,256,128]{4,3,2,1,0:T(8,128)(2,1)}, u32[]{:S(2)}) copy-start(bf16[1,32,1,256,128]{4,3,2,1,0:T(8,128)(2,1)} %param.17) | copy-start | bytes 6291460
  4.7 3.3 %copy-start.1 = (bf16[1,6144,256]{2,1,0:T(8,128)(2,1)S(1)}, bf16[1,6144,256]{2,1,0:T(8,128)(2,1)}, u32[]{:S(2)}) copy-start(bf16[1,6144,256]{2,1,0:T(8,128)(2,1)} %param.25) | copy-start | bytes 9437188
  5.5 2.6 %copy-start.2 = (bf16[768,384]{1,0:T(8,128)(2,1)S(1)}, bf16[768,384]{1,0:T(8,128)(2,1)}, u32[]{:S(2)}) copy-start(bf16[768,384]{1,0:T(8,128)(2,1)} %proj_hbm.1) | copy-start | bytes 1769476
  5.5 2.6 %copy-start.3 = (bf16[1,512,384]{2,1,0:T(8,128)(2,1)S(1)}, bf16[1,512,384]{2,1,0:T(8,128)(2,1)}, u32[]{:S(2)}) copy-start(bf16[1,512,384]{2,1,0:T(8,128)(2,1)} %param.21) | copy-start | bytes 1179652
  5.5 2.6 %copy-start.4 = (s32[2,512,2]{1,2,0:T(2,128)S(1)}, s32[2,512,2]{1,2,0:T(2,128)}, u32[]{:S(2)}) copy-start(s32[2,512,2]{1,2,0:T(2,128)} %param.23) | copy-start | bytes 24580
  5.5 2.6 %copy-start.5 = (f32[2,512,2]{1,2,0:T(2,128)S(1)}, f32[2,512,2]{1,2,0:T(2,128)}, u32[]{:S(2)}) copy-start(f32[2,512,2]{1,2,0:T(2,128)} %param.24) | copy-start | bytes 24580

commit v2 on v1

v2 whole, which is shorter than its diff:
```python
import math

import jax
import jax.numpy as jnp
from jax import lax
from jax.experimental import pallas as pl
from jax.experimental.pallas import tpu as pltpu
from jax.sharding import PartitionSpec as P

MESH = pl.DeviceIdType.MESH
BF16 = jnp.bfloat16
F32 = jnp.float32
D = 6144
SIDE = 4
GROUPS = 16
PLANES = 8
ROWS = 128


def remote(src, dst, send_sem, recv_sem, device):
    return pltpu.make_async_remote_copy(
        src_ref=src,
        dst_ref=dst,
        send_sem=send_sem,
        recv_sem=recv_sem,
        device_id=device,
        device_id_type=MESH,
    )


class Torus:
    def __init__(self, role, x, y, plane):
        self.role, self.plane = role, plane
        self.xs = [lax.rem(x + k, SIDE) * SIDE for k in range(SIDE)]
        self.ys = [lax.rem(y + k, SIDE) for k in range(SIDE)]

    def at(self, half, first, second):
        dx, dy = (first, second) if half == 0 else (second, first)
        return self.xs[dx] + self.ys[dy]

    def device(self, half, first, second):
        return (self.role, self.at(half, first, second), self.plane)


class PlaneGather:
    def __init__(self, torus, blocks, piece, send, recv):
        self.torus, self.blocks, self.piece, self.send, self.recv = torus, blocks, piece, send, recv

    def copy(self, half, first, phase, step):
        piece = self.piece(self.torus.at(half, first, 0), half)
        if phase == 0:
            target = self.torus.device(half, step, 0)
            recv = self.recv.at[half * SIDE + SIDE - step]
        else:
            target = self.torus.device(half, 0, step)
            recv = self.recv.at[2 * SIDE + (first if half == 0 else SIDE - step)]
        return remote(piece, piece, self.send, recv, target)

    def taken(self, ref, which):
        remote(ref, ref, self.send, self.recv.at[which], self.torus.device(0, 1, 0)).wait_recv()

    def start(self):
        for phase in range(2):
            for step in (1, 3, 2):
                for half in (0, 1):
                    self.copy(half, 0, phase, step).start()

    def forward(self):
        for first in (1, 3, 2):
            for half in (0, 1):
                self.taken(self.piece(self.torus.at(half, first, 0), half), half * SIDE + first)
                for step in (1, 3, 2):
                    self.copy(half, first, 1, step).start()

    def row(self, dx, halves):
        self.taken(self.blocks(halves), 2 * SIDE + dx)

    def finish(self):
        ref = self.blocks(30)
        remote(ref, ref, self.send, self.recv.at[0], self.torus.device(0, 1, 0)).wait_send()


class RelayGather:
    def __init__(self, torus, blocks, piece, send, recv):
        self.torus, self.blocks, self.piece, self.send, self.recv = torus, blocks, piece, send, recv

    def first_axis(self, half, step):
        piece = self.piece(self.torus.at(half, 0, 0), half, None)
        recv = self.recv.at[SIDE - step]
        remote(piece, piece, self.send, recv, self.torus.device(half, step, 0)).start()

    def second_axis(self, half, first, step):
        piece = self.piece(self.torus.at(half, first, 0), half, None)
        recv = self.recv.at[SIDE + 2 * first + (SIDE - step) // 2]
        remote(piece, piece, self.send, recv, self.torus.device(half, 0, step)).start()

    def pass_on(self, half, first, side):
        piece = self.piece(self.torus.at(half, first, side), half, side // 2)
        recv = self.recv.at[3 * SIDE + first]
        remote(piece, piece, self.send, recv, self.torus.device(half, 0, SIDE - side)).start()

    def taken(self, which):
        ref = self.blocks(1)
        remote(ref, ref, self.send, self.recv.at[which], self.torus.device(0, 1, 0)).wait_recv()

    def start(self):
        for step in (1, 3, 2):
            for half in (0, 1):
                self.first_axis(half, step)
        for step in (1, 3):
            for half in (0, 1):
                self.second_axis(half, 0, step)

    def turn(self):
        for first in (1, 3, 2):
            self.taken(first)
            for step in (1, 3):
                for half in (0, 1):
                    self.second_axis(half, first, step)

    def relay(self, first):
        for side in (1, 3):
            self.taken(SIDE + 2 * first + side // 2)
            for half in (0, 1):
                self.pass_on(half, first, side)

    def far(self):
        for first in (0, 1, 3, 2):
            self.taken(3 * SIDE + first)

    def finish(self):
        ref = self.blocks(15)
        remote(ref, ref, self.send, self.recv.at[0], self.torus.device(0, 1, 0)).wait_send()


def near_side(i):
    return i + i // 2


def attend(query_ref, key_ref, value_ref, lengths_ref, keys, values, arrive, spread_q, fresh_kv, scores, mixed, out):
    factor = 1.0 / math.sqrt(128)
    spread_q[...] = jnp.zeros_like(spread_q)
    query = query_ref[...].astype(F32)
    fresh_kv[0] = key_ref[...].astype(F32)
    fresh_kv[1] = value_ref[...].astype(F32)
    for head in range(6):
        spread_q[:, head, :] = query[:, head * 128 : head * 128 + 128]
    position = lax.broadcasted_iota(jnp.int32, (8, 256), 1)

    def group(i, carry):
        some = pl.ds(i * 8, 8)
        arrive(0, i)
        for k in range(8):
            s = i * 8 + k
            raw = lax.dot_general(
                spread_q[s].astype(BF16),
                keys[s],
                (((1,), (1,)), ((), ())),
                preferred_element_type=F32,
            )
            scores[s] = jnp.where(position < lengths_ref[0, s], raw * factor, -jnp.inf)
        rows = pl.ds(pl.multiple_of(i * 8, 8), 8)
        fresh_key = fresh_kv[0, rows, :][:, None, :]
        fresh = jnp.sum(spread_q[some] * fresh_key, axis=-1, keepdims=True) * factor
        score = scores[some]
        highest = jnp.maximum(jnp.max(score, axis=-1, keepdims=True), fresh)
        weights = jnp.exp(score - highest)
        own = jnp.exp(fresh - highest)
        denominator = jnp.sum(weights, axis=-1, keepdims=True) + own
        probs = (weights / denominator).astype(BF16)
        own_prob = (own / denominator).astype(BF16).astype(F32)
        fresh_value = fresh_kv[1, rows, :][:, None, :]
        own_part = own_prob * fresh_value
        arrive(1, i)
        for k in range(8):
            s = i * 8 + k
            mixed[s] = jnp.dot(probs[k], values[s], preferred_element_type=F32) + own_part[k]
        return carry

    lax.fori_loop(0, 4, group, 0)
    for head in range(6):
        out[:, head * 128 : head * 128 + 128] = mixed[:, head, :].astype(BF16)


def layer(
    lengths_ref,
    query_hbm,
    new_key_hbm,
    new_value_hbm,
    keys_hbm,
    values_hbm,
    proj_hbm,
    resid_hbm,
    gain_hbm,
    ids_hbm,
    gates_hbm,
    gate_hbm,
    up_hbm,
    down_hbm,
    stream_ref,
    mix_ref,
    query,
    new_key,
    new_value,
    keys,
    values,
    spread_q,
    fresh_kv,
    scores,
    mixed,
    attn_mine,
    attn_all,
    proj,
    resid_ref,
    gain_ref,
    ids_ref,
    gates_ref,
    gate_w,
    up_w,
    down_w,
    heads,
    head_in,
    rows_all,
    gate_acc,
    up_acc,
    square_acc,
    hidden_all,
    down_acc,
    half_out,
    half_in,
    mix_part,
    mix_in,
    pick,
    place_t,
    weight_col,
    load_sem,
    cache_sem,
    attn_send,
    attn_recv,
    rows_send,
    rows_recv,
    hid_send,
    hid_recv,
    sib_send,
    sib_recv,
    swap_send,
    swap_recv,
    z_send,
    z_recv,
):
    role = lax.axis_index("role")
    grp = lax.axis_index("grp")
    plane = lax.axis_index("tp")
    x, y = grp // SIDE, lax.rem(grp, SIDE)
    torus = Torus(role, x, y, plane)
    sibling = (1 - role, grp, plane)

    def along_z(step):
        return (role, grp, lax.rem(plane + step, PLANES))

    barrier = pltpu.get_barrier_semaphore()
    near = [(role, lax.rem(x + k, SIDE) * SIDE + y, plane) for k in (1, 2, 3)]
    near += [(role, x * SIDE + lax.rem(y + k, SIDE), plane) for k in (1, 2, 3)]
    near += [along_z(k) for k in range(1, PLANES)] + [sibling]
    for device in near:
        pl.semaphore_signal(barrier, inc=1, device_id=device, device_id_type=MESH)

    pairs = (
        (query_hbm, query),
        (new_key_hbm, new_key),
        (new_value_hbm, new_value),
        (ids_hbm, ids_ref),
        (gates_hbm, gates_ref),
        (gain_hbm, gain_ref),
        (proj_hbm, proj),
        (resid_hbm, resid_ref),
        (gate_hbm, gate_w),
        (up_hbm, up_w),
        (down_hbm, down_w),
    )
    loads = [pltpu.make_async_copy(src, dst, load_sem.at[i]) for i, (src, dst) in enumerate(pairs)]

    def cache_load(which, i):
        src, dst = ((keys_hbm, keys), (values_hbm, values))[which]
        some = pl.ds(i * 8, 8)
        return pltpu.make_async_copy(src.at[some], dst.at[some], cache_sem.at[which, i])

    for load in loads[:3]:
        load.start()
    for i in range(4):
        cache_load(0, i).start()
        cache_load(1, i).start()
    for load in loads[3:]:
        load.start()
    for load in loads[:3]:
        load.wait()
    attend(
        query,
        new_key,
        new_value,
        lengths_ref,
        keys,
        values,
        lambda which, i: cache_load(which, i).wait(),
        spread_q,
        fresh_kv,
        scores,
        mixed,
        attn_mine,
    )
    attn_all[pl.ds(grp * 32, 32), :] = attn_mine[...]
    pl.semaphore_wait(barrier, len(near))

    attn = PlaneGather(
        torus,
        lambda halves: attn_all.at[pl.ds(0, halves * 16)],
        lambda g, half: attn_all.at[pl.ds(g * 32 + half * 16, 16)],
        attn_send.at[0],
        attn_recv,
    )
    attn.start()

    for load in loads[3:8]:
        load.wait()
    ids = ids_ref[role]
    hit0, hit1 = ids[0:1, :] == plane, ids[1:2, :] == plane
    named = jnp.where(hit0 | hit1, 1.0, 0.0)
    gates = gates_ref[role]
    weight_row = jnp.where(hit0, gates[0:1, :], gates[1:2, :])
    seqs = named.shape[1]
    slots = pick.shape[0]
    earlier = lax.broadcasted_iota(jnp.int32, (seqs, seqs), 0) < lax.broadcasted_iota(
        jnp.int32, (seqs, seqs), 1
    )
    before = jnp.dot(
        jnp.broadcast_to(named, (16, seqs)).astype(BF16),
        jnp.where(earlier, 1.0, 0.0).astype(BF16),
        preferred_element_type=F32,
    )[0:1, :]
    slot = jnp.where(named > 0.5, before, -1.0).astype(jnp.int32)
    chosen = jnp.where(slot == lax.broadcasted_iota(jnp.int32, (slots, seqs), 0), 1.0, 0.0)
    pick[...] = chosen.astype(BF16)

    attn.forward()

    place_t[...] = chosen.T.astype(BF16)
    weight_col[...] = jnp.broadcast_to(
        jnp.sum(chosen * weight_row, axis=1, keepdims=True), weight_col.shape
    )
    gate_acc[...] = jnp.zeros_like(gate_acc)
    up_acc[...] = jnp.zeros_like(up_acc)
    square_acc[...] = jnp.zeros_like(square_acc)
    down_acc[...] = jnp.zeros_like(down_acc)

    mine = pl.ds(plane * 64, 64)

    def part_for(src, dst, s, step):
        to = lax.rem(plane + step, PLANES)
        sems = z_send.at[s], z_recv.at[s]
        return remote(src.at[pl.ds(to * 64, 64)], dst.at[step], *sems, along_z(step))

    def seven(ref, s):
        ref = ref.at[pl.ds(0, 7 * 64)]
        return remote(ref, ref, z_send.at[s], z_recv.at[s], along_z(1))

    def project(dx):
        row = lax.rem(x + dx, SIDE)
        some = pl.ds(row * 128, 128)
        part = jnp.dot(attn_all[some, :], proj[...], preferred_element_type=F32)
        heads[some, :] = part.astype(BF16)
        for k in range(2):
            step = lax.rem(2 * row + k + PLANES - plane, PLANES)

            @pl.when(step != 0)
            def _():
                part_for(heads, head_in, 0, step).start()

    attn.row(0, 3)
    project(0)

    def attn_rest(i, carry):
        dx = jnp.where(i == 2, 2, 2 * i + 1)
        attn.row(dx, 7)
        project(dx)
        return carry

    lax.fori_loop(0, 3, attn_rest, 0)

    def collect(src, dst, s):
        seven(src, s).wait_recv()

        def add(step, carry):
            return carry + dst[step].astype(F32)

        return lax.fori_loop(1, PLANES, add, src[mine, :].astype(F32))

    def spread(ref, s):
        def go(step, carry):
            block = ref.at[mine]
            remote(block, block, z_send.at[s], z_recv.at[s], along_z(step)).start()
            return carry

        lax.fori_loop(1, PLANES, go, 0)
        seven(ref, s).wait_recv()

    summed = collect(heads, head_in, 0)
    stream_ref[mine, :] = (resid_ref[mine, :].astype(F32) + summed).astype(BF16)
    spread(stream_ref, 1)

    def gain_of(g):
        return jnp.concatenate([gain_ref[pl.ds(g * 3 + k, 1), :] for k in range(3)], axis=1)

    scaled = (stream_ref[...].astype(F32) * gain_of(grp)).astype(BF16)
    rows = []
    for k in range(2):
        some = pl.ds(k * ROWS, ROWS)
        rows_all[role, grp, some, :] = jnp.dot(
            pick[some, :], scaled, preferred_element_type=F32
        ).astype(BF16)

        def rows_piece(g, half, part, k=k):
            start = k * ROWS + half * 64 + 32 * (part or 0)
            return rows_all.at[role, g, pl.ds(start, 64 if part is None else 32)]

        def rows_blocks(count, k=k):
            return rows_all.at[role, pl.ds(0, count), pl.ds(k * ROWS, ROWS)]

        rows.append(RelayGather(torus, rows_blocks, rows_piece, rows_send.at[k], rows_recv.at[k]))
        rows[k].start()

    def block_at(dx, dy):
        return lax.rem(x + dx, SIDE) * SIDE + lax.rem(y + dy, SIDE)

    def share(k, group, dx, dy):
        block = rows_all.at[role, block_at(dx, dy), pl.ds(k * ROWS, ROWS)]
        remote(block, block, sib_send.at[0], sib_recv.at[k, group], sibling).start()

    def shared(k, group, count):
        ref = rows_all.at[1 - role, pl.ds(0, count), pl.ds(k * ROWS, ROWS)]
        remote(ref, ref, sib_send.at[0], sib_recv.at[k, group], sibling).wait_recv()

    def expert_in(k, dx, dy):
        g = block_at(dx, dy)
        depth = pl.ds(pl.multiple_of(g * 384, 128), 384)
        block = rows_all[:, g, pl.ds(k * ROWS, ROWS), :].reshape(2 * ROWS, 384)
        gate_acc[k] += jnp.dot(block, gate_w[depth, :], preferred_element_type=F32)
        up_acc[k] += jnp.dot(block, up_w[depth, :], preferred_element_type=F32)
        plain = block.astype(F32) * (1.0 / gain_of(g))
        plain = plain * plain
        square_acc[k] += plain[:, :128] + plain[:, 128:256] + plain[:, 256:]

    def beside(i):
        a = 1 + 2 * lax.rem(i, 2)
        return jnp.where(i < 2, a, 0), jnp.where(i < 2, 0, a)

    def across(i):
        return 1 + 2 * (i // 2), 1 + 2 * lax.rem(i, 2)

    def far(i):
        return (
            jnp.where(i < 3, 2, jnp.where(i < 6, near_side(i - 3), 2)),
            jnp.where(i < 3, near_side(i), 2),
        )

    def each(count, where, one):
        def body(i, carry):
            one(*where(i))
            return carry

        lax.fori_loop(0, count, body, 0)

    def share_all(k, group, count, where):
        each(count, where, lambda dx, dy: share(k, group, dx, dy))

    def enter(k, group, count, where):
        shared(k, group, count)
        each(count, where, lambda dx, dy: expert_in(k, dx, dy))

    hid = []

    def hidden(k):
        mean = jnp.sum(square_acc[k], axis=1, keepdims=True) / D
        rstat = 1.0 / jnp.sqrt(mean + 1e-05)
        act = gate_acc[k] * rstat
        hidden_all[k, grp] = (act / (1.0 + jnp.exp(-act)) * (up_acc[k] * rstat)).astype(BF16)

        def piece(g, half, part):
            start = half * ROWS + 64 * (part or 0)
            return hidden_all.at[k, g, pl.ds(start, ROWS if part is None else 64)]

        hid.append(
            RelayGather(
                torus,
                lambda count: hidden_all.at[k, pl.ds(0, count)],
                piece,
                hid_send.at[k],
                hid_recv.at[k],
            )
        )
        hid[k].start()

    def expert_out(k, dx, dy):
        g = block_at(dx, dy)
        depth = pl.ds(pl.multiple_of(g * 256, 256), 256)
        down_acc[k] += jnp.dot(hidden_all[k, g], down_w[depth, :], preferred_element_type=F32)

    def swap(k):
        some = pl.ds(k * ROWS, ROWS)
        sems = swap_send.at[k], swap_recv.at[k]
        return remote(half_out.at[some], half_in.at[some], *sems, sibling)

    def leave(k, count, where):
        each(count, where, lambda dx, dy: expert_out(k, dx, dy))

    def leave_near(k):
        expert_out(k, 0, 0)
        leave(k, 4, beside)
        leave(k, 4, across)

    def leave_far(k):
        hid[k].far()
        leave(k, 7, far)
        theirs = down_acc[k, pl.ds((1 - role) * ROWS, ROWS), :]
        half_out[pl.ds(k * ROWS, ROWS), :] = theirs.astype(BF16)
        swap(k).start()

    for k in range(2):
        share(k, 0, 0, 0)
    for k in range(2):
        rows[k].turn()
    loads[8].wait()
    loads[9].wait()
    for k in range(2):
        shared(k, 0, 1)
        expert_in(k, 0, 0)
    for k in range(2):
        rows[k].relay(0)
        share_all(k, 1, 4, beside)
    for k in range(2):
        rows[k].relay(1)
        share(k, 2, 1, 1)
    enter(0, 1, 4, beside)
    for k in range(2):
        rows[k].relay(3)
        share(k, 2, 1, 3)
        share(k, 2, 3, 1)
        share(k, 2, 3, 3)
    enter(1, 1, 4, beside)
    for k in range(2):
        rows[k].relay(2)
    enter(0, 2, 4, across)
    rows[0].far()
    share_all(0, 3, 7, far)
    enter(1, 2, 4, across)
    enter(0, 3, 7, far)
    hidden(0)
    rows[1].far()
    share_all(1, 3, 7, far)
    loads[10].wait()
    enter(1, 3, 7, far)
    hidden(1)
    for k in range(2):
        hid[k].turn()
    for first in (0, 1, 3, 2):
        hid[0].relay(first)
    leave_near(0)
    for first in (0, 1):
        hid[1].relay(first)
    leave_far(0)
    for first in (3, 2):
        hid[1].relay(first)
    leave_near(1)
    leave_far(1)

    weighted = []
    for k in range(2):
        swap(k).wait_recv()
        some = pl.ds(k * ROWS, ROWS)
        whole = down_acc[k, pl.ds(role * ROWS, ROWS), :] + half_in[some, :].astype(F32)
        weighted.append((whole * weight_col[some, 0:1]).astype(BF16))
    weighted = jnp.concatenate(weighted, axis=0)
    mix_part[...] = jnp.dot(place_t[...], weighted, preferred_element_type=F32).astype(BF16)

    def mix_go(step, carry):
        part_for(mix_part, mix_in, 2, step).start()
        return carry

    lax.fori_loop(1, PLANES, mix_go, 0)
    mix_ref[mine, :] = collect(mix_part, mix_in, 2).astype(BF16)
    spread(mix_ref, 3)

    attn.finish()
    for k in range(2):
        rows[k].finish()
        hid[k].finish()
        swap(k).wait_send()

    for i, ref in enumerate((heads, stream_ref, mix_part, mix_ref)):
        seven(ref, i).wait_send()
    everything = rows_all.at[role]
    remote(everything, everything, sib_send.at[0], sib_recv.at[0, 0], sibling).wait_send()


def local(
    queries,
    new_keys,
    new_values,
    cache_keys,
    cache_values,
    lengths,
    out_proj,
    residual,
    norm_gain,
    expert_ids,
    gate_weights,
    expert_gate,
    expert_up,
    expert_down,
):
    vmem = pl.BlockSpec(memory_space=pltpu.VMEM)
    hbm = pl.BlockSpec(memory_space=pl.ANY)
    dma = pltpu.SemaphoreType.DMA
    stream, mix = pl.pallas_call(
        layer,
        out_shape=(
            jax.ShapeDtypeStruct((512, 384), BF16),
            jax.ShapeDtypeStruct((512, 384), BF16),
        ),
        in_specs=[pl.BlockSpec(memory_space=pltpu.SMEM)] + [hbm] * 13,
        out_specs=(vmem, vmem),
        scratch_shapes=[
            pltpu.VMEM((32, 768), BF16),
            pltpu.VMEM((32, 128), BF16),
            pltpu.VMEM((32, 128), BF16),
            pltpu.VMEM((32, 256, 128), BF16),
            pltpu.VMEM((32, 256, 128), BF16),
            pltpu.VMEM((32, 8, 128), F32),
            pltpu.VMEM((2, 32, 128), F32),
            pltpu.VMEM((32, 8, 256), F32),
            pltpu.VMEM((32, 8, 128), F32),
            pltpu.VMEM((32, 768), BF16),
            pltpu.VMEM((512, 768), BF16),
            pltpu.VMEM((768, 384), BF16),
            pltpu.VMEM((512, 384), BF16),
            pltpu.VMEM((48, 128), F32),
            pltpu.VMEM((2, 2, 512), jnp.int32),
            pltpu.VMEM((2, 2, 512), F32),
            pltpu.VMEM((6144, 256), BF16),
            pltpu.VMEM((6144, 256), BF16),
            pltpu.VMEM((4096, 384), BF16),
            pltpu.VMEM((512, 384), BF16),
            pltpu.VMEM((8, 64, 384), BF16),
            pltpu.VMEM((2, 16, 256, 384), BF16),
            pltpu.VMEM((2, 256, 256), F32),
            pltpu.VMEM((2, 256, 256), F32),
            pltpu.VMEM((2, 256, 128), F32),
            pltpu.VMEM((2, 16, 256, 256), BF16),
            pltpu.VMEM((2, 256, 384), F32),
            pltpu.VMEM((256, 384), BF16),
            pltpu.VMEM((256, 384), BF16),
            pltpu.VMEM((512, 384), BF16),
            pltpu.VMEM((8, 64, 384), BF16),
            pltpu.VMEM((256, 512), BF16),
            pltpu.VMEM((512, 256), BF16),
            pltpu.VMEM((256, 128), F32),
            dma((11,)),
            dma((2, 4)),
            dma((1,)),
            dma((12,)),
            dma((2,)),
            dma((2, 16)),
            dma((2,)),
            dma((2, 16)),
            dma((1,)),
            dma((2, 4)),
            dma((2,)),
            dma((2,)),
            dma((4,)),
            dma((4,)),
        ],
        compiler_params=pltpu.CompilerParams(
            collective_id=0, has_side_effects=True, vmem_limit_bytes=56 << 20
        ),
    )(
        lengths,
        queries[0],
        new_keys[0],
        new_values[0],
        cache_keys.reshape(32, 256, 128),
        cache_values.reshape(32, 256, 128),
        out_proj,
        residual[0],
        norm_gain.reshape(48, 128),
        jnp.swapaxes(expert_ids, 1, 2),
        jnp.swapaxes(gate_weights, 1, 2),
        expert_gate[0],
        expert_up[0],
        expert_down[0],
    )
    return (stream[None], mix[None])


def solution(mesh):
    return jax.shard_map(
        local,
        mesh=mesh,
        in_specs=(
            P("role", "grp", "tp"),
            P("role", "grp", "tp"),
            P("role", "grp", "tp"),
            P("role", "grp", "tp", None, None),
            P("role", "grp", "tp", None, None),
            P("role", "grp"),
            P("tp", "grp"),
            P("role", None, "grp"),
            P(),
            P(),
            P(),
            P("tp", None, ("role", "grp")),
            P("tp", None, ("role", "grp")),
            P("tp", "role", "grp"),
        ),
        out_specs=(P("role", None, "grp"), P("role", None, "grp")),
        check_vma=False,
    )
```

time: 142 us -> 124 us (0.87); the launches traced: 140 us -> 124 us
  Pallas kernels: 131 us -> 120 us
  matrix products: 3.9 us -> 0 us
  other arithmetic: 1.79 us -> 0 us
    pallas_call x1, Pallas kernels: 131 us -> 120 us  [local(): pl.pallas_call(layer, out_shape=(jax.ShapeDtypeStruct((512, 384), BF16),...]
    dot_general x3 -> x0, matrix products: 3.9 us -> none  [the longest x1 2.31 us: attend_local(): jnp.einsum('skgp,skpd->skgd', probs, cache_values[0], preferred_element_t...]
    unnamed x15 -> x2, local copies, waits for them, and re-layouts: 1.55 us -> 3.56 us
where the time goes in v2:
time: 124 us
  Pallas kernels  120 us (97%)
  local copies, waits for them, and re-layouts  3.56 us (3%)
    pallas_call x1, Pallas kernels, local(): pl.pallas_call(layer, out_shape=(jax.ShapeDtypeStruct((512, 384), BF16),...  120 us
    unnamed x2, local copies, waits for them, and re-layouts  3.56 us

profile of v2, /device:TPU:1, one launch (start us, length us, event | category | flops | bytes accessed | tf_op | source)
XLA Modules:
  0.0 123.9 jit_solution(9498825892790785570)
XLA Ops:
  0.6 119.7 %shard_map.149 = (bf16[512,384]{1,0:T(8,128)(2,1)}, bf16[512,384]{1,0:T(8,128)(2,1)}) custom-call(s32[1,32]{1,0:T(1,128)} %lengths_ref.1, bf16[32,768]{1,0:T(8,128)(2,1)} %bitcast.22, bf16[32,128]{1,0:T(8,128)(2,1)} %bitcast.24, bf16[32,128]{1,0:T(8,128)(2,1)} %bitcast.25, bf16[32,256,128]{2,1,0:T(8,128)(2,1)} %bitcast.17, bf16[32,256,128]{2,1,0:T(8,128)(2,1)} %bitcast.18, ...), custom_call_target="tpu_custom_call" | custom-call | tf_op jit(solution)/shard_map/pallas_call | solution.py:623
  120.4 1.8 %copy.18 = bf16[1,512,384]{2,1,0:T(8,128)(2,1)} copy(bf16[1,512,384]{2,1,0:T(8,128)(2,1)} %bitcast.20) | data formatting | bytes 786432
  122.1 1.8 %copy.19 = bf16[1,512,384]{2,1,0:T(8,128)(2,1)} copy(bf16[1,512,384]{2,1,0:T(8,128)(2,1)} %bitcast.19) | data formatting | bytes 786432

commit v3 on v2

--- a/solution.py
+++ b/solution.py
@@ -14,7 +14,7 @@
 SIDE = 4
 GROUPS = 16
 PLANES = 8
-ROWS = 128
+FARTHEST_FIRST = (4, 3, 5, 2, 6, 1, 7)
 
 
 def remote(src, dst, send_sem, recv_sem, device):
@@ -104,7 +104,7 @@
         remote(ref, ref, self.send, self.recv.at[which], self.torus.device(0, 1, 0)).wait_recv()
 
     def start(self):
-        for step in (1, 3, 2):
+        for step in (2, 1, 3):
             for half in (0, 1):
                 self.first_axis(half, step)
         for step in (1, 3):
@@ -124,9 +124,8 @@
             for half in (0, 1):
                 self.pass_on(half, first, side)
 
-    def far(self):
-        for first in (0, 1, 3, 2):
-            self.taken(3 * SIDE + first)
+    def far(self, first):
+        self.taken(3 * SIDE + first)
 
     def finish(self):
         ref = self.blocks(15)
@@ -183,7 +182,7 @@
 
 
 def layer(
-    lengths_ref,
+    lengths_hbm,
     query_hbm,
     new_key_hbm,
     new_value_hbm,
@@ -199,6 +198,7 @@
     down_hbm,
     stream_ref,
     mix_ref,
+    lengths_ref,
     query,
     new_key,
     new_value,
@@ -259,13 +259,15 @@
         return (role, grp, lax.rem(plane + step, PLANES))
 
     barrier = pltpu.get_barrier_semaphore()
-    near = [(role, lax.rem(x + k, SIDE) * SIDE + y, plane) for k in (1, 2, 3)]
-    near += [(role, x * SIDE + lax.rem(y + k, SIDE), plane) for k in (1, 2, 3)]
-    near += [along_z(k) for k in range(1, PLANES)] + [sibling]
+    near = [along_z(k) for k in FARTHEST_FIRST]
+    near += [(role, lax.rem(x + k, SIDE) * SIDE + y, plane) for k in (2, 1, 3)]
+    near += [(role, x * SIDE + lax.rem(y + k, SIDE), plane) for k in (2, 1, 3)]
+    near += [sibling]
     for device in near:
         pl.semaphore_signal(barrier, inc=1, device_id=device, device_id_type=MESH)
 
     pairs = (
+        (lengths_hbm, lengths_ref),
         (query_hbm, query),
         (new_key_hbm, new_key),
         (new_value_hbm, new_value),
@@ -285,14 +287,14 @@
         some = pl.ds(i * 8, 8)
         return pltpu.make_async_copy(src.at[some], dst.at[some], cache_sem.at[which, i])
 
-    for load in loads[:3]:
+    for load in loads[:4]:
         load.start()
     for i in range(4):
         cache_load(0, i).start()
         cache_load(1, i).start()
-    for load in loads[3:]:
+    for load in loads[4:]:
         load.start()
-    for load in loads[:3]:
+    for load in loads[:4]:
         load.wait()
     attend(
         query,
@@ -320,7 +322,7 @@
     )
     attn.start()
 
-    for load in loads[3:8]:
+    for load in loads[4:9]:
         load.wait()
     ids = ids_ref[role]
     hit0, hit1 = ids[0:1, :] == plane, ids[1:2, :] == plane
@@ -395,12 +397,9 @@
         return lax.fori_loop(1, PLANES, add, src[mine, :].astype(F32))
 
     def spread(ref, s):
-        def go(step, carry):
-            block = ref.at[mine]
+        block = ref.at[mine]
+        for step in FARTHEST_FIRST:
             remote(block, block, z_send.at[s], z_recv.at[s], along_z(step)).start()
-            return carry
-
-        lax.fori_loop(1, PLANES, go, 0)
         seven(ref, s).wait_recv()
 
     summed = collect(heads, head_in, 0)
@@ -411,43 +410,38 @@
         return jnp.concatenate([gain_ref[pl.ds(g * 3 + k, 1), :] for k in range(3)], axis=1)
 
     scaled = (stream_ref[...].astype(F32) * gain_of(grp)).astype(BF16)
-    rows = []
-    for k in range(2):
-        some = pl.ds(k * ROWS, ROWS)
-        rows_all[role, grp, some, :] = jnp.dot(
-            pick[some, :], scaled, preferred_element_type=F32
-        ).astype(BF16)
-
-        def rows_piece(g, half, part, k=k):
-            start = k * ROWS + half * 64 + 32 * (part or 0)
-            return rows_all.at[role, g, pl.ds(start, 64 if part is None else 32)]
-
-        def rows_blocks(count, k=k):
-            return rows_all.at[role, pl.ds(0, count), pl.ds(k * ROWS, ROWS)]
-
-        rows.append(RelayGather(torus, rows_blocks, rows_piece, rows_send.at[k], rows_recv.at[k]))
-        rows[k].start()
+    rows_all[role, grp] = jnp.dot(pick[...], scaled, preferred_element_type=F32).astype(BF16)
+    rows = RelayGather(
+        torus,
+        lambda count: rows_all.at[role, pl.ds(0, count)],
+        lambda g, half, part: rows_all.at[
+            role, g, pl.ds(half * 128 + 64 * (part or 0), 128 if part is None else 64)
+        ],
+        rows_send.at[0],
+        rows_recv,
+    )
+    rows.start()
 
     def block_at(dx, dy):
         return lax.rem(x + dx, SIDE) * SIDE + lax.rem(y + dy, SIDE)
 
-    def share(k, group, dx, dy):
-        block = rows_all.at[role, block_at(dx, dy), pl.ds(k * ROWS, ROWS)]
-        remote(block, block, sib_send.at[0], sib_recv.at[k, group], sibling).start()
-
-    def shared(k, group, count):
-        ref = rows_all.at[1 - role, pl.ds(0, count), pl.ds(k * ROWS, ROWS)]
-        remote(ref, ref, sib_send.at[0], sib_recv.at[k, group], sibling).wait_recv()
-
-    def expert_in(k, dx, dy):
+    def share(group, dx, dy):
+        block = rows_all.at[role, block_at(dx, dy)]
+        remote(block, block, sib_send.at[0], sib_recv.at[group], sibling).start()
+
+    def shared(group, count):
+        ref = rows_all.at[1 - role, pl.ds(0, count)]
+        remote(ref, ref, sib_send.at[0], sib_recv.at[group], sibling).wait_recv()
+
+    def expert_in(dx, dy):
         g = block_at(dx, dy)
         depth = pl.ds(pl.multiple_of(g * 384, 128), 384)
-        block = rows_all[:, g, pl.ds(k * ROWS, ROWS), :].reshape(2 * ROWS, 384)
-        gate_acc[k] += jnp.dot(block, gate_w[depth, :], preferred_element_type=F32)
-        up_acc[k] += jnp.dot(block, up_w[depth, :], preferred_element_type=F32)
+        block = rows_all[:, g].reshape(512, 384)
+        gate_acc[...] += jnp.dot(block, gate_w[depth, :], preferred_element_type=F32)
+        up_acc[...] += jnp.dot(block, up_w[depth, :], preferred_element_type=F32)
         plain = block.astype(F32) * (1.0 / gain_of(g))
         plain = plain * plain
-        square_acc[k] += plain[:, :128] + plain[:, 128:256] + plain[:, 256:]
+        square_acc[...] += plain[:, :128] + plain[:, 128:256] + plain[:, 256:]
 
     def beside(i):
         a = 1 + 2 * lax.rem(i, 2)
@@ -469,136 +463,113 @@
 
         lax.fori_loop(0, count, body, 0)
 
-    def share_all(k, group, count, where):
-        each(count, where, lambda dx, dy: share(k, group, dx, dy))
-
-    def enter(k, group, count, where):
-        shared(k, group, count)
-        each(count, where, lambda dx, dy: expert_in(k, dx, dy))
-
-    hid = []
-
-    def hidden(k):
-        mean = jnp.sum(square_acc[k], axis=1, keepdims=True) / D
-        rstat = 1.0 / jnp.sqrt(mean + 1e-05)
-        act = gate_acc[k] * rstat
-        hidden_all[k, grp] = (act / (1.0 + jnp.exp(-act)) * (up_acc[k] * rstat)).astype(BF16)
-
-        def piece(g, half, part):
-            start = half * ROWS + 64 * (part or 0)
-            return hidden_all.at[k, g, pl.ds(start, ROWS if part is None else 64)]
-
-        hid.append(
-            RelayGather(
-                torus,
-                lambda count: hidden_all.at[k, pl.ds(0, count)],
-                piece,
-                hid_send.at[k],
-                hid_recv.at[k],
-            )
-        )
-        hid[k].start()
-
-    def expert_out(k, dx, dy):
+    def share_all(group, count, where):
+        each(count, where, lambda dx, dy: share(group, dx, dy))
+
+    def enter(group, count, where):
+        shared(group, count)
+        each(count, where, expert_in)
+
+    share(0, 0, 0)
+    rows.turn()
+    loads[9].wait()
+    loads[10].wait()
+    shared(0, 1)
+    expert_in(0, 0)
+    def far_pair(i, first):
+        shared(3 + i, 2)
+        expert_in(first, 2)
+        expert_in(2, first)
+
+    rows.relay(0)
+    share_all(1, 4, beside)
+    enter(1, 4, beside)
+    rows.relay(1)
+    share(2, 1, 1)
+    rows.relay(3)
+    share(2, 1, 3)
+    share(2, 3, 1)
+    share(2, 3, 3)
+    rows.relay(2)
+    for i, first in enumerate((0, 1, 3, 2)):
+        rows.far(first)
+        if first == 2:
+            share(3 + i, 2, 2)
+        else:
+            share(3 + i, first, 2)
+            share(3 + i, 2, first)
+        if i == 0:
+            enter(2, 4, across)
+        else:
+            far_pair(i - 1, (0, 1, 3)[i - 1])
+    shared(6, 1)
+    expert_in(2, 2)
+
+    hid = RelayGather(
+        torus,
+        lambda count: hidden_all.at[pl.ds(0, count)],
+        lambda g, half, part: hidden_all.at[
+            g, pl.ds(half * 256 + 128 * (part or 0), 256 if part is None else 128)
+        ],
+        hid_send.at[0],
+        hid_recv,
+    )
+    mean = jnp.sum(square_acc[...], axis=1, keepdims=True) / D
+    rstat = 1.0 / jnp.sqrt(mean + 1e-05)
+    act = gate_acc[...] * rstat
+    hidden_all[grp] = (act / (1.0 + jnp.exp(-act)) * (up_acc[...] * rstat)).astype(BF16)
+    hid.start()
+
+    def expert_out(dx, dy):
         g = block_at(dx, dy)
         depth = pl.ds(pl.multiple_of(g * 256, 256), 256)
-        down_acc[k] += jnp.dot(hidden_all[k, g], down_w[depth, :], preferred_element_type=F32)
-
-    def swap(k):
-        some = pl.ds(k * ROWS, ROWS)
-        sems = swap_send.at[k], swap_recv.at[k]
-        return remote(half_out.at[some], half_in.at[some], *sems, sibling)
-
-    def leave(k, count, where):
-        each(count, where, lambda dx, dy: expert_out(k, dx, dy))
-
-    def leave_near(k):
-        expert_out(k, 0, 0)
-        leave(k, 4, beside)
-        leave(k, 4, across)
-
-    def leave_far(k):
-        hid[k].far()
-        leave(k, 7, far)
-        theirs = down_acc[k, pl.ds((1 - role) * ROWS, ROWS), :]
-        half_out[pl.ds(k * ROWS, ROWS), :] = theirs.astype(BF16)
-        swap(k).start()
-
-    for k in range(2):
-        share(k, 0, 0, 0)
-    for k in range(2):
-        rows[k].turn()
-    loads[8].wait()
-    loads[9].wait()
-    for k in range(2):
-        shared(k, 0, 1)
-        expert_in(k, 0, 0)
-    for k in range(2):
-        rows[k].relay(0)
-        share_all(k, 1, 4, beside)
-    for k in range(2):
-        rows[k].relay(1)
-        share(k, 2, 1, 1)
-    enter(0, 1, 4, beside)
-    for k in range(2):
-        rows[k].relay(3)
-        share(k, 2, 1, 3)
-        share(k, 2, 3, 1)
-        share(k, 2, 3, 3)
-    enter(1, 1, 4, beside)
-    for k in range(2):
-        rows[k].relay(2)
-    enter(0, 2, 4, across)
-    rows[0].far()
-    share_all(0, 3, 7, far)
-    enter(1, 2, 4, across)
-    enter(0, 3, 7, far)
-    hidden(0)
-    rows[1].far()
-    share_all(1, 3, 7, far)
-    loads[10].wait()
-    enter(1, 3, 7, far)
-    hidden(1)
-    for k in range(2):
-        hid[k].turn()
-    for first in (0, 1, 3, 2):
-        hid[0].relay(first)
-    leave_near(0)
-    for first in (0, 1):
-        hid[1].relay(first)
-    leave_far(0)
-    for first in (3, 2):
-        hid[1].relay(first)
-    leave_near(1)
-    leave_far(1)
-
-    weighted = []
-    for k in range(2):
-        swap(k).wait_recv()
-        some = pl.ds(k * ROWS, ROWS)
-        whole = down_acc[k, pl.ds(role * ROWS, ROWS), :] + half_in[some, :].astype(F32)
-        weighted.append((whole * weight_col[some, 0:1]).astype(BF16))
-    weighted = jnp.concatenate(weighted, axis=0)
+        down_acc[...] += jnp.dot(hidden_all[g], down_w[depth, :], preferred_element_type=F32)
+
+    hid.turn()
+    loads[11].wait()
+    expert_out(0, 0)
+    hid.relay(0)
+    each(4, beside, expert_out)
+    for first in (1, 3, 2):
+        hid.relay(first)
+    each(4, across, expert_out)
+    hid.far(0)
+    expert_out(0, 2)
+    expert_out(2, 0)
+    for first in (1, 3):
+        hid.far(first)
+        expert_out(first, 2)
+        expert_out(2, first)
+    hid.far(2)
+    expert_out(2, 2)
+    half_out[...] = down_acc[pl.ds((1 - role) * 256, 256), :].astype(BF16)
+    swap = remote(half_out, half_in, swap_send.at[0], swap_recv.at[0], sibling)
+    swap.start()
+
+    swap.wait_recv()
+    whole = down_acc[pl.ds(role * 256, 256), :] + half_in[...].astype(F32)
+    weighted = (whole * weight_col[:, 0:1]).astype(BF16)
     mix_part[...] = jnp.dot(place_t[...], weighted, preferred_element_type=F32).astype(BF16)
 
-    def mix_go(step, carry):
+    for step in FARTHEST_FIRST:
         part_for(mix_part, mix_in, 2, step).start()
-        return carry
-
-    lax.fori_loop(1, PLANES, mix_go, 0)
+    attn.finish()
+    rows.finish()
+    hid.finish()
+    for i, ref in ((0, heads), (1, stream_ref)):
+        seven(ref, i).wait_send()
+    everything = rows_all.at[role]
+    remote(everything, everything, sib_send.at[0], sib_recv.at[0], sibling).wait_send()
     mix_ref[mine, :] = collect(mix_part, mix_in, 2).astype(BF16)
     spread(mix_ref, 3)
-
-    attn.finish()
-    for k in range(2):
-        rows[k].finish()
-        hid[k].finish()
-        swap(k).wait_send()
-
-    for i, ref in enumerate((heads, stream_ref, mix_part, mix_ref)):
+    swap.wait_send()
+    for i, ref in ((2, mix_part), (3, mix_ref)):
         seven(ref, i).wait_send()
-    everything = rows_all.at[role]
-    remote(everything, everything, sib_send.at[0], sib_recv.at[0, 0], sibling).wait_send()
+
+
+def hand_over(stream_ref, mix_ref, stream_out, mix_out):
+    stream_out[0] = stream_ref[...]
+    mix_out[0] = mix_ref[...]
 
 
 def local(
@@ -626,9 +597,10 @@
             jax.ShapeDtypeStruct((512, 384), BF16),
             jax.ShapeDtypeStruct((512, 384), BF16),
         ),
-        in_specs=[pl.BlockSpec(memory_space=pltpu.SMEM)] + [hbm] * 13,
+        in_specs=[hbm] * 14,
         out_specs=(vmem, vmem),
         scratch_shapes=[
+            pltpu.SMEM((1, 32), jnp.int32),
             pltpu.VMEM((32, 768), BF16),
             pltpu.VMEM((32, 128), BF16),
             pltpu.VMEM((32, 128), BF16),
@@ -651,11 +623,11 @@
             pltpu.VMEM((512, 384), BF16),
             pltpu.VMEM((8, 64, 384), BF16),
             pltpu.VMEM((2, 16, 256, 384), BF16),
-            pltpu.VMEM((2, 256, 256), F32),
-            pltpu.VMEM((2, 256, 256), F32),
-            pltpu.VMEM((2, 256, 128), F32),
-            pltpu.VMEM((2, 16, 256, 256), BF16),
-            pltpu.VMEM((2, 256, 384), F32),
+            pltpu.VMEM((512, 256), F32),
+            pltpu.VMEM((512, 256), F32),
+            pltpu.VMEM((512, 128), F32),
+            pltpu.VMEM((16, 512, 256), BF16),
+            pltpu.VMEM((512, 384), F32),
             pltpu.VMEM((256, 384), BF16),
             pltpu.VMEM((256, 384), BF16),
             pltpu.VMEM((512, 384), BF16),
@@ -663,18 +635,18 @@
             pltpu.VMEM((256, 512), BF16),
             pltpu.VMEM((512, 256), BF16),
             pltpu.VMEM((256, 128), F32),
-            dma((11,)),
+            dma((12,)),
             dma((2, 4)),
             dma((1,)),
             dma((12,)),
-            dma((2,)),
-            dma((2, 16)),
-            dma((2,)),
-            dma((2, 16)),
             dma((1,)),
-            dma((2, 4)),
-            dma((2,)),
-            dma((2,)),
+            dma((16,)),
+            dma((1,)),
+            dma((16,)),
+            dma((1,)),
+            dma((7,)),
+            dma((1,)),
+            dma((1,)),
             dma((4,)),
             dma((4,)),
         ],
@@ -697,7 +669,12 @@
         expert_up[0],
         expert_down[0],
     )
-    return (stream[None], mix[None])
+    return pl.pallas_call(
+        hand_over,
+        out_shape=(jax.ShapeDtypeStruct((1, 512, 384), BF16),) * 2,
+        in_specs=[vmem, vmem],
+        out_specs=(vmem, vmem),
+    )(stream, mix)
 
 
 def solution(mesh):

time: 124 us -> 115 us (0.927)
  Pallas kernels: 120 us -> 114 us
  local copies, waits for them, and re-layouts: 3.56 us -> 0 us
    pallas_call x1, Pallas kernels: 120 us -> 112 us  [local(): pl.pallas_call(layer, out_shape=(jax.ShapeDtypeStruct((512, 384), BF16),...]
    unnamed x2 -> x0, local copies, waits for them, and re-layouts: 3.56 us -> none
    pallas_call x0 -> x1, Pallas kernels: none -> 2.03 us  [local(): pl.pallas_call(hand_over, out_shape=(jax.ShapeDtypeStruct((1, 512, 384),...]
where the time goes in v3:
time: 115 us
  Pallas kernels  114 us (99%)
    pallas_call x1, Pallas kernels, local(): pl.pallas_call(layer, out_shape=(jax.ShapeDtypeStruct((512, 384), BF16),...  112 us

profile of v3, /device:TPU:1, one launch (start us, length us, event | category | flops | bytes accessed | tf_op | source)
XLA Modules:
  0.0 114.9 jit_solution(5642376453593028121)
XLA Ops:
  0.6 112.2 %shard_map.149 = (bf16[512,384]{1,0:T(8,128)(2,1)}, bf16[512,384]{1,0:T(8,128)(2,1)}) custom-call(s32[1,32]{1,0:T(1,128)} %lengths_hbm.1, bf16[32,768]{1,0:T(8,128)(2,1)} %bitcast.18, bf16[32,128]{1,0:T(8,128)(2,1)} %bitcast.20, bf16[32,128]{1,0:T(8,128)(2,1)} %bitcast.21, bf16[32,256,128]{2,1,0:T(8,128)(2,1)} %bitcast.15, bf16[32,256,128]{2,1,0:T(8,128)(2,1)} %bitcast.16, ...), custom_call_target="tpu_custom_call" | custom-call | tf_op jit(solution)/shard_map/pallas_call | solution.py:594
  112.9 2.0 %shard_map.150 = (bf16[1,512,384]{2,1,0:T(8,128)(2,1)}, bf16[1,512,384]{2,1,0:T(8,128)(2,1)}) custom-call(bf16[512,384]{1,0:T(8,128)(2,1)} %get-tuple-element.4.stream_ref, bf16[512,384]{1,0:T(8,128)(2,1)} %get-tuple-element.5.mix_ref), custom_call_target="tpu_custom_call" | custom-call | tf_op jit(solution)/shard_map/pallas_call | solution.py:672

commit v4 on v3

--- a/solution.py
+++ b/solution.py
@@ -61,7 +61,7 @@
 
     def start(self):
         for phase in range(2):
-            for step in (1, 3, 2):
+            for step in (2, 1, 3):
                 for half in (0, 1):
                     self.copy(half, 0, phase, step).start()
 
@@ -69,7 +69,7 @@
         for first in (1, 3, 2):
             for half in (0, 1):
                 self.taken(self.piece(self.torus.at(half, first, 0), half), half * SIDE + first)
-                for step in (1, 3, 2):
+                for step in (2, 1, 3):
                     self.copy(half, first, 1, step).start()
 
     def row(self, dx, halves):
@@ -94,6 +94,11 @@
         recv = self.recv.at[SIDE + 2 * first + (SIDE - step) // 2]
         remote(piece, piece, self.send, recv, self.torus.device(half, 0, step)).start()
 
+    def pass_first(self, half, side):
+        piece = self.piece(self.torus.at(half, side, 0), half, side // 2)
+        target = self.torus.device(half, SIDE - side, 0)
+        remote(piece, piece, self.send, self.recv.at[2], target).start()
+
     def pass_on(self, half, first, side):
         piece = self.piece(self.torus.at(half, first, side), half, side // 2)
         recv = self.recv.at[3 * SIDE + first]
@@ -104,7 +109,7 @@
         remote(ref, ref, self.send, self.recv.at[which], self.torus.device(0, 1, 0)).wait_recv()
 
     def start(self):
-        for step in (2, 1, 3):
+        for step in (1, 3):
             for half in (0, 1):
                 self.first_axis(half, step)
         for step in (1, 3):
@@ -114,6 +119,8 @@
     def turn(self):
         for first in (1, 3, 2):
             self.taken(first)
+            for half in (0, 1) if first != 2 else ():
+                self.pass_first(half, first)
             for step in (1, 3):
                 for half in (0, 1):
                     self.second_axis(half, first, step)

time: 115 us -> 114 us (level)
  no operation moved by 1% of the time
where the time goes in v4:
time: 114 us
  Pallas kernels  113 us (99%)
    pallas_call x1, Pallas kernels, local(): pl.pallas_call(layer, out_shape=(jax.ShapeDtypeStruct((512, 384), BF16),...  111 us

profile of v4, /device:TPU:1, one launch (start us, length us, event | category | flops | bytes accessed | tf_op | source)
XLA Modules:
  0.0 114.1 jit_solution(16390043675505074650)
XLA Ops:
  0.6 111.4 %shard_map.149 = (bf16[512,384]{1,0:T(8,128)(2,1)}, bf16[512,384]{1,0:T(8,128)(2,1)}) custom-call(s32[1,32]{1,0:T(1,128)} %lengths_hbm.1, bf16[32,768]{1,0:T(8,128)(2,1)} %bitcast.18, bf16[32,128]{1,0:T(8,128)(2,1)} %bitcast.20, bf16[32,128]{1,0:T(8,128)(2,1)} %bitcast.21, bf16[32,256,128]{2,1,0:T(8,128)(2,1)} %bitcast.15, bf16[32,256,128]{2,1,0:T(8,128)(2,1)} %bitcast.16, ...), custom_call_target="tpu_custom_call" | custom-call | tf_op jit(solution)/shard_map/pallas_call | solution.py:601
  112.1 2.0 %shard_map.150 = (bf16[1,512,384]{2,1,0:T(8,128)(2,1)}, bf16[1,512,384]{2,1,0:T(8,128)(2,1)}) custom-call(bf16[512,384]{1,0:T(8,128)(2,1)} %get-tuple-element.4.stream_ref, bf16[512,384]{1,0:T(8,128)(2,1)} %get-tuple-element.5.mix_ref), custom_call_target="tpu_custom_call" | custom-call | tf_op jit(solution)/shard_map/pallas_call | solution.py:679
